TPU v7x, 512 devices: a whole 4x4x16 slice. The times are simulated.
512 devices in a mesh: chan: 64 (over x_hi, z, core), tm: 8 (over x_lo, y).
Axes of the slice: x: 4 (x_hi: 2, x_lo: 2; x = x_hi * 2 + x_lo), y: 4, z: 16, core: 2. Of those that a mesh axis runs over, the one named last changes fastest.
Arguments:
- traces: bfloat16 [6144, 65536], P('chan', 'tm'), may hold values from -6 to 6
- live_channels: int32 [64], P('chan'), may hold values from 48 to 96
- partners: int32 [64, 3], P('chan'), may hold values from -1 to 63, as said below
Outputs:
- lags: float32 [6144, 3, 1024], P('chan', None, 'tm')
Inputs may be any that keep to these rules, and one draw needn't show every extreme that they name: `partners`: row a lists distinct blocks b with a < b <= a + 3 and b < 64, ascending, then -1 in the empty slots. Block 0 lists all 3; the last block lists none.
All inputs are finite; a program needn't handle non-finite values.
Results may differ from a plain program's by a relative error of at most 0.0064.
Values may be sent and summed in bfloat16 or wider, within the bound.
A program may use at most 128 MiB of HBM per device.

v0:
```python
import math

import jax
import jax.numpy as jnp
from jax import lax
from jax.sharding import PartitionSpec as P

NFFT = 1024
SMOOTH = 64
LIMIT = 3


def from_behind(x, axis, by):
    devices = lax.axis_size(axis)
    pairs = [(i, i + by) for i in range(devices) if 0 <= i + by < devices]
    return lax.ppermute(x, axis, pairs)


def hann_taper(length):
    steps = jnp.arange(length, dtype=jnp.float32)
    return 0.5 - 0.5 * jnp.cos(steps * (2.0 * math.pi / length))


def forward_table(length):
    half = length // 2
    samples = jnp.arange(length, dtype=jnp.int32)[:, None]
    freqs = jnp.arange(1, half + 1, dtype=jnp.int32)[None, :]
    phase = (samples * freqs % length).astype(jnp.float32) * (2.0 * math.pi / length)
    return jnp.concatenate([jnp.cos(phase), -jnp.sin(phase)], 1).astype(jnp.bfloat16)


def band_matrix(half, window):
    source = jnp.arange(half, dtype=jnp.int32)[:, None]
    target = jnp.arange(half, dtype=jnp.int32)[None, :]
    start = jnp.clip(target - window // 2, 0, half - window)
    return ((source >= start) & (source < start + window)).astype(jnp.float32)


def lag_table(length, first, count):
    half = length // 2
    freqs = jnp.arange(1, half + 1, dtype=jnp.int32)[:, None]
    shifts = (first + jnp.arange(count, dtype=jnp.int32))[None, :]
    phase = (freqs * shifts % length).astype(jnp.float32) * (2.0 * math.pi / length)
    weight = jnp.where(freqs < half, 2.0, 1.0).astype(jnp.float32) / math.sqrt(length)
    return jnp.concatenate([weight * jnp.cos(phase), -weight * jnp.sin(phase)], 0)


def whiten(extended, length):
    hop = length // 2
    chans = extended.shape[0]
    segs = extended.shape[1] // hop - 1
    first = extended[:, : segs * hop].reshape(chans, segs, hop)
    second = extended[:, hop:].reshape(chans, segs, hop)
    pieces = jnp.concatenate([first, second], 2)
    tapered = (pieces.astype(jnp.float32) * hann_taper(length)).astype(jnp.bfloat16)
    spectra = jnp.dot(
        tapered.reshape(-1, length), forward_table(length), preferred_element_type=jnp.float32
    )
    real_part = spectra[:, :hop]
    imag_part = spectra[:, hop:]
    power = real_part * real_part + imag_part * imag_part
    smooth = jnp.dot(power, band_matrix(hop, SMOOTH), precision=lax.Precision.HIGHEST) / SMOOTH
    factor = lax.rsqrt(smooth + 1e-06)
    white = (spectra * jnp.concatenate([factor, factor], 1)).astype(jnp.bfloat16)
    return white.reshape(chans, segs, length)


def cross_stack(own, partner):
    hop = own.shape[2] // 2
    own_re = own[:, :, :hop].astype(jnp.float32)
    own_im = own[:, :, hop:].astype(jnp.float32)
    par_re = partner[:, :, :hop].astype(jnp.float32)
    par_im = partner[:, :, hop:].astype(jnp.float32)
    real_sum = jnp.sum(own_re * par_re + own_im * par_im, axis=1)
    imag_sum = jnp.sum(own_im * par_re - own_re * par_im, axis=1)
    return jnp.concatenate([real_sum, imag_sum], 1)


def per_device(traces, live_channels, partners):
    chans = traces.shape[0]
    length = NFFT
    hop = length // 2
    alive = jnp.arange(chans, dtype=jnp.int32) < live_channels[0]
    masked = jnp.where(alive[:, None], traces, jnp.zeros_like(traces))
    tail = from_behind(masked[:, :hop], "tm", -1)
    extended = jnp.concatenate([masked, tail], 1)
    own_white = whiten(extended, length)
    copies = []
    for offset in range(LIMIT):
        copies.append(from_behind(own_white, "chan", -(offset + 1)))
    gathered = jnp.stack(copies)
    block = lax.axis_index("chan")
    rows = []
    for slot in range(LIMIT):
        target = partners[0, slot]
        reach = jnp.clip(target - block - 1, 0, LIMIT - 1)
        partner = lax.dynamic_index_in_dim(gathered, reach, 0, keepdims=False)
        rows.append(jnp.where(target >= 0, cross_stack(own_white, partner), jnp.float32(0.0)))
    local = jnp.stack(rows, 1)
    count = own_white.shape[1] * lax.axis_size("tm")
    total = lax.psum(local, "tm")
    columns = length // lax.axis_size("tm")
    table = lag_table(length, lax.axis_index("tm") * columns, columns)
    result = jnp.dot((total / count).reshape(-1, length), table, precision=lax.Precision.HIGHEST)
    return result.reshape(chans, LIMIT, columns)


def solution(mesh):
    in_specs = (P("chan", "tm"), P("chan"), P("chan", None))
    out_specs = P("chan", None, "tm")
    return jax.shard_map(
        per_device, mesh=mesh, in_specs=in_specs, out_specs=out_specs, check_vma=False
    )
```

profile of v0, /device:TPU:1, one launch (start us, length us, event | category | flops | bytes accessed | tf_op | source)
XLA Modules:
  0.0 365.5 jit_solution(6905639850178751996)
XLA Ops:
  7.2 1.6 broadcast_select_fusion
  8.8 1.3 collective-permute-start
  10.1 2.1 concatenate.63
  12.3 9.4 %cosine_convert_fusion = (bf16[1024,512]{1,0:T(8,128)(2,1)}, bf16[1024,512]{1,0:T(8,128)(2,1)}) fusion(s32[512]{0:T(512)S(1)} %iota_add_fusion), kind=kLoop, calls=%fused_computation.52 | loop fusion | flops 8912896 | bytes 2099200 | tf_op jit(solution)/shard_map/convert
  21.7 0.1 pad_maximum_fusion.1
  21.8 0.8 concatenate.65
  22.6 5.4 %fusion.3 = f32[1536,1024]{1,0:T(8,128)S(1)} fusion(bf16[1536,512]{1,0:T(8,128)(2,1)S(1)} %concatenate.65, bf16[1536,512]{1,0:T(8,128)(2,1)} %concatenate.63, f32[1024]{0:T(1024)S(1)} %multiply_subtract_fusion, bf16[1024,512]{1,0:T(8,128)(2,1)} %get-tuple-element.23, bf16[1024,512]{1,0:T(8,128)(2,1)} %get-tuple-element.22), kind=kOutput, calls=%fused_computation.19 | convolution fusion | flops 3234856960 | bytes 11538432 | tf_op jit(solution)/shard_map/dot_general | solution.py:56
  28.0 3.0 fusion.2
  31.0 1.6 fusion
  32.7 8.8 %collective-permute-start.1 = (bf16[96,16,1024]{2,1,0:T(8,128)(2,1)S(1)}, bf16[96,16,1024]{2,1,0:T(8,128)(2,1)}, u32[]{:S(2)}, u32[]{:S(2)}) collective-permute-start(bf16[96,16,1024]{2,1,0:T(8,128)(2,1)S(1)} %bitcast.24), channel_id=1, source_target_pairs={{8,0},{16,8},{24,16},{32,24},{40,32},{48,40},{56,48},{64,56},{72,6... | collective-permute-start | bytes 9437192 | tf_op jit(solution)/shard_map/ppermute | solution.py:16
  41.5 1.3 collective-permute-start.2
  42.8 1.5 collective-permute-start.3
  44.3 0.7 fusion.47
  48.9 50.5 %collective-permute-done.1 = bf16[96,16,1024]{2,1,0:T(8,128)(2,1)} collective-permute-done((bf16[96,16,1024]{2,1,0:T(8,128)(2,1)S(1)}, bf16[96,16,1024]{2,1,0:T(8,128)(2,1)}, u32[]{:S(2)}, u32[]{:S(2)}) %collective-permute-start.1) | collective-permute-done | bytes 3145760 | tf_op jit(solution)/shard_map/ppermute | solution.py:16
  99.4 14.3 %collective-permute-done.2 = bf16[96,16,1024]{2,1,0:T(8,128)(2,1)} collective-permute-done((bf16[96,16,1024]{2,1,0:T(8,128)(2,1)S(1)}, bf16[96,16,1024]{2,1,0:T(8,128)(2,1)}, u32[]{:S(2)}, u32[]{:S(2)}) %collective-permute-start.2) | collective-permute-done | bytes 3145760 | tf_op jit(solution)/shard_map/ppermute | solution.py:16
  113.7 128.9 %collective-permute-done.3 = bf16[96,16,1024]{2,1,0:T(8,128)(2,1)} collective-permute-done((bf16[96,16,1024]{2,1,0:T(8,128)(2,1)S(1)}, bf16[96,16,1024]{2,1,0:T(8,128)(2,1)}, u32[]{:S(2)}, u32[]{:S(2)}) %collective-permute-start.3) | collective-permute-done | bytes 3145760 | tf_op jit(solution)/shard_map/ppermute | solution.py:16
  242.6 4.6 %pad_maximum_fusion = bf16[3,96,16,1024]{3,2,1,0:T(8,128)(2,1)S(1)} fusion(bf16[1,96,16,1024]{3,2,1,0:T(8,128)(2,1)} %bitcast.5, bf16[1,96,16,1024]{3,2,1,0:T(8,128)(2,1)} %bitcast.4, bf16[1,96,16,1024]{3,2,1,0:T(8,128)(2,1)} %bitcast.3), kind=kLoop, calls=%fused_computation | loop fusion | flops 9437184 | bytes 18874368 | tf_op jit(solution)/shard_map/stack | solution.py:91
  247.2 4.5 %dynamic-slice_bitcast_fusion.1 = (bf16[96,16,1024]{2,1,0:T(8,128)(2,1)}, bf16[96,16,1024]{2,1,0:T(8,128)(2,1)}, bf16[96,16,1024]{2,1,0:T(8,128)(2,1)}) fusion(bf16[3,96,16,1024]{3,2,1,0:T(8,128)(2,1)S(1)} %pad_maximum_fusion, s32[]{:T(128)S(6)} %min.21, s32[]{:T(128)S(6)} %min.22, s32[]{:T(128)S(6)} %min.20), kind=kLoop, calls=%fused_computation.39 | loop fusion | bytes 18874380 | tf_op jit(solution)/shard_map/jit(dynamic_index_in_dim)/squeeze | solution.py:97
  251.7 10.5 %fusion.9 = (f32[96,512]{1,0:T(8,128)S(1)}, f32[96,512]{1,0:T(8,128)S(1)}, f32[96,512]{1,0:T(8,128)S(1)}, f32[96,512]{1,0:T(8,128)S(1)}, f32[96,512]{1,0:T(8,128)S(1)}, /*index=5*/f32[96,512]{1,0:T(8,128)S(1)}) fusion(bf16[96,16,1024]{2,1,0:T(8,128)(2,1)} %get-tuple-element.13, bf16[96,16,1024]{2,1,0:T(8,128)(2,1)S(1)} %bitcast.27, ...), kind=kLoop, calls=%fused_computation.25 | loop fusion | flops 24870912 | bytes 13762560 | tf_op jit(solution)/shard_map/reduce_sum | solution.py:74
  262.4 1.2 pad_maximum_fusion.2
  263.5 0.0 all-reduce.2.cloned.1.call-update
  263.6 1.1 cosine_multiply_fusion
  264.7 90.9 %all-reduce.2.cloned.1.call-done = f32[96,3,1024]{2,0,1:T(8,128)} async-done(((f32[96,3,1024]{2,0,1:T(8,128)}), f32[96,3,1024]{2,0,1:T(8,128)}) %all-reduce.2.cloned.1.call-update) | async-done | bytes 1179664 | tf_op jit(solution)/shard_map/psum | solution.py:101
  355.7 3.0 fusion.31
  (14 shorter events, 0.2 us)
Async XLA Ops:
  6.5 349.1 %all-reduce.2.cloned.1.call-start = ((), (), s32[]{:S(2)}) async-start(), calls=%async_computation | async-start | bytes 2359296 | tf_op jit(solution)/shard_map/psum | solution.py:101
  8.8 12.9 %collective-permute-start = (bf16[96,512]{1,0:T(8,128)(2,1)S(1)}, bf16[96,512]{1,0:T(8,128)(2,1)S(1)}, u32[]{:S(2)}, u32[]{:S(2)}) collective-permute-start(bf16[96,512]{1,0:T(8,128)(2,1)S(1)} %slice.64), channel_id=1, source_target_pairs={{1,0},{2,1},{3,2},{4,3},{5,4},{6,5},{7,6},{9,8},{10,9},{11,10},{12... | collective-permute-start | bytes 294920 | tf_op jit(solution)/shard_map/ppermute | solution.py:16
  31.0 13.2 %copy-start = (s32[1,3]{1,0:T(1,128)S(1)}, s32[1,3]{1,0:T(1,128)}, u32[]{:S(2)}) copy-start(s32[1,3]{1,0:T(1,128)} %param.5) | copy-start | bytes 40
  32.7 66.7 %collective-permute-start.1 = (bf16[96,16,1024]{2,1,0:T(8,128)(2,1)S(1)}, bf16[96,16,1024]{2,1,0:T(8,128)(2,1)}, u32[]{:S(2)}, u32[]{:S(2)}) collective-permute-start(bf16[96,16,1024]{2,1,0:T(8,128)(2,1)S(1)} %bitcast.24), channel_id=1, source_target_pairs={{8,0},{16,8},{24,16},{32,24},{40,32},{48,40},{56,48},{64,56},{72,6... | collective-permute-start | bytes 9437192 | tf_op jit(solution)/shard_map/ppermute | solution.py:16
  41.5 72.2 %collective-permute-start.2 = (bf16[96,16,1024]{2,1,0:T(8,128)(2,1)S(1)}, bf16[96,16,1024]{2,1,0:T(8,128)(2,1)}, u32[]{:S(2)}, u32[]{:S(2)}) collective-permute-start(bf16[96,16,1024]{2,1,0:T(8,128)(2,1)S(1)} %bitcast.25), channel_id=1, source_target_pairs={{16,0},{24,8},{32,16},{40,24},{48,32},{56,40},{64,48},{72,56},{80,... | collective-permute-start | bytes 9437192 | tf_op jit(solution)/shard_map/ppermute | solution.py:16
  42.8 199.8 %collective-permute-start.3 = (bf16[96,16,1024]{2,1,0:T(8,128)(2,1)S(1)}, bf16[96,16,1024]{2,1,0:T(8,128)(2,1)}, u32[]{:S(2)}, u32[]{:S(2)}) collective-permute-start(bf16[96,16,1024]{2,1,0:T(8,128)(2,1)S(1)} %bitcast.26), channel_id=1, source_target_pairs={{24,0},{32,8},{40,16},{48,24},{56,32},{64,40},{72,48},{80,56},{88,... | collective-permute-start | bytes 9437192 | tf_op jit(solution)/shard_map/ppermute | solution.py:16
Sparse Core Ops, SparseCore 0:
  263.7 91.9 all-reduce.1
where the time goes:
time: 370 us; the launch traced here: 366 us
  waiting for transfers between devices  285 us (77%)
  other arithmetic  30.3 us (8%)
  between operations  18.1 us (5%)
  starting transfers between devices  12.8 us (3%)
  matrix products  11.5 us (3%)
  local copies, waits for them, and re-layouts  8.11 us (2%)
    ppermute x4, waiting for transfers between devices, from_behind(): return lax.ppermute(x, axis, pairs)  194 us
    psum x1, waiting for transfers between devices, per_device(): total = lax.psum(local, 'tm')  90.9 us
    ppermute x4, starting transfers between devices, from_behind(): return lax.ppermute(x, axis, pairs)  12.8 us
    reduce_sum x1, other arithmetic, cross_stack(): real_sum = jnp.sum(own_re * par_re + own_im * par_im, axis=1)  10.5 us
    another operation x1, other arithmetic  9.39 us
  transfers between devices with their start and end apart: 5, of which 4 were waited for; matrix products, arithmetic and copies ran while one was open for 4% of the time, Pallas kernels for 0%

commit v1 on v0

v1 whole, which is shorter than its diff:
```python
import functools
import math

import jax
import jax.numpy as jnp
import ml_dtypes
import numpy as np
from jax import lax
from jax.experimental import pallas as pl
from jax.experimental.pallas import tpu as pltpu
from jax.sharding import PartitionSpec as P

NFFT = 1024
HOP = NFFT // 2
SMOOTH = 64
LIMIT = 3
MESH = pl.DeviceIdType.MESH
F32 = jnp.float32
BF16 = jnp.bfloat16

SLOT_A, SLOT_B, SLOT_C, SLOT_D, SLOT_E = range(5)
PAIRS = 6


def bin_order():
    return np.concatenate([np.arange(2, HOP + 1, 2), np.arange(1, HOP, 2)])


def taper_rows():
    steps = np.arange(NFFT, dtype=np.float64)
    return (0.5 - 0.5 * np.cos(steps * (2.0 * math.pi / NFFT))).astype(np.float32).reshape(2, HOP)


def forward_tables():
    samples = np.arange(HOP)[:, None]
    tables = []
    for bins in (bin_order()[None, : HOP // 2], bin_order()[None, HOP // 2 :]):
        phase = (samples * bins % NFFT) * (2.0 * math.pi / NFFT)
        tables.append(np.concatenate([np.cos(phase), -np.sin(phase)], 1))
    return np.stack(tables).astype(ml_dtypes.bfloat16)


def band_table():
    freqs = bin_order() - 1
    start = np.clip(freqs - SMOOTH // 2, 0, HOP - SMOOTH)[None, :]
    source = freqs[:, None]
    return (((source >= start) & (source < start + SMOOTH)) / SMOOTH).astype(ml_dtypes.bfloat16)


def lag_tables(segments):
    shifts = np.arange(HOP)[None, :]
    tables = []
    for bins in (bin_order()[: HOP // 2, None], bin_order()[HOP // 2 :, None]):
        phase = (bins * shifts % NFFT) * (2.0 * math.pi / NFFT)
        weight = np.where(bins < HOP, 2.0, 1.0) / math.sqrt(NFFT) / segments
        tables.append(np.concatenate([weight * np.cos(phase), -weight * np.sin(phase)], 0))
    return np.stack(tables).astype(ml_dtypes.bfloat16)


def chunk_bounds(segs):
    bounds = [(4 * s + 1, 4 * s + 5) for s in range(segs // 4)]
    bounds[0] = (0, 5)
    bounds[-1] = (bounds[-1][0], segs)
    return bounds


def kernel(
    nq, nt, segs, chans,
    live_hbm, partners_hbm, x_ref, taper_hbm, fwd_hbm, band_hbm, lag_hbm, out_ref,
    live, partners, taper, own, buf, white, acc, fwd, band, lagt, part, gath, fin, res,
    load_sem, table_sem, ssem, rsem, hsend, hrecv, asend, arecv, fsend, frecv,
):
    half = chans // 2
    steps = segs // 4
    cols = NFFT // nt
    chunks = chunk_bounds(segs)
    chan = lax.axis_index("chan")
    t = lax.axis_index("tm")
    q = chan // 2
    c = lax.rem(chan, 2)
    below, above = q > 0, q < nq - 1
    mine = SLOT_B + c
    theirs = SLOT_C - c

    def at(chip, core, time):
        return {"chan": 2 * chip + core, "tm": time}

    for h in range(segs):
        pltpu.make_async_copy(x_ref.at[:, pl.ds(HOP * h, HOP)], own.at[h], load_sem.at[h]).start()
    tables = [
        pltpu.make_async_copy(fwd_hbm, fwd, table_sem.at[0]),
        pltpu.make_async_copy(band_hbm, band, table_sem.at[1]),
        pltpu.make_async_copy(lag_hbm, lagt, table_sem.at[2]),
        pltpu.make_async_copy(taper_hbm, taper, table_sem.at[3]),
        pltpu.make_async_copy(partners_hbm, partners, table_sem.at[4]),
    ]
    live_copy = pltpu.make_async_copy(live_hbm, live, table_sem.at[5])
    live_copy.start()
    for copy in tables:
        copy.start()

    @pl.when(q == 0)
    def _():
        buf[SLOT_A] = jnp.zeros((segs + 1, half, HOP), BF16)

    @pl.when(q == nq - 1)
    def _():
        buf[SLOT_D] = jnp.zeros((segs + 1, half, HOP), BF16)
        buf[SLOT_E] = jnp.zeros((segs + 1, half, HOP), BF16)
        res[...] = jnp.zeros(res.shape, F32)

    @pl.when(t == nt - 1)
    def _():
        for slot in range(5):
            buf[slot, segs] = jnp.zeros((half, HOP), BF16)

    barrier = pltpu.get_barrier_semaphore()

    def greet(chip, core, time):
        pl.semaphore_signal(barrier, inc=1, device_id=at(chip, core, time), device_id_type=MESH)

    for d in range(1, nt):
        greet(q, c, lax.rem(t + d, nt))

    def greet_around(time):
        greet(q, 1 - c, time)

        @pl.when(below)
        def _():
            greet(q - 1, 0, time)
            greet(q - 1, 1, time)

        @pl.when(above)
        def _():
            greet(q + 1, 0, time)
            greet(q + 1, 1, time)

    greet_around(t)

    @pl.when(t > 0)
    def _():
        greet_around(t - 1)

    @pl.when(t < nt - 1)
    def _():
        greet_around(t + 1)

    live_copy.wait()
    alive = lax.broadcasted_iota(jnp.int32, (chans, HOP), 0) < live[0]
    mask = jnp.where(alive, F32(1.0), F32(0.0)).astype(BF16)

    def mask_one(h, carry):
        pltpu.make_async_copy(
            x_ref.at[:, pl.ds(pl.multiple_of(HOP * h, HOP), HOP)], own.at[h], load_sem.at[h]
        ).wait()
        own[h] = own[h] * mask
        buf[mine, h] = own[h, pl.ds(pl.multiple_of(half * c, half), half), :]
        return carry

    lax.fori_loop(0, segs, mask_one, 0)

    around = 1 + 2 * jnp.where(below, 1, 0) + 2 * jnp.where(above, 1, 0)
    times = 1 + jnp.where(t > 0, 1, 0) + jnp.where(t < nt - 1, 1, 0)
    pl.semaphore_wait(barrier, nt - 1 + around * times)

    outward = 2 * c - 1
    main_ok = jnp.where(c == 0, q, nq - 1 - q) > 0
    edge_ok = c * q > 0

    def route(index):
        if index == 0:
            return half * (1 - c), mine, q, 1 - c
        if index in (1, 2):
            return half * (index - 1), 3 * (1 - c), q + outward, index - 1
        if index in (3, 4):
            return half * (index - 3), SLOT_E, q - 1, index - 3
        return half * c, mine, q, c

    def stream(index, k):
        lo, hi = chunks[k]
        row, slot, chip, core = route(index)
        return pltpu.make_async_remote_copy(
            src_ref=own.at[pl.ds(lo, hi - lo), pl.ds(row, half), :],
            dst_ref=buf.at[slot, pl.ds(lo, hi - lo)],
            send_sem=ssem.at[index, k],
            recv_sem=rsem.at[slot, k],
            device_id=at(chip, core, t),
            device_id_type=MESH,
        )

    def halo(index):
        row, slot, chip, core = route(index)
        return pltpu.make_async_remote_copy(
            src_ref=own.at[0, pl.ds(row, half), :],
            dst_ref=buf.at[slot, segs],
            send_sem=hsend.at[index],
            recv_sem=hrecv.at[slot],
            device_id=at(chip, core, t - 1),
            device_id_type=MESH,
        )

    def halos(act):
        @pl.when(t > 0)
        def _():
            act(halo(5))
            act(halo(0))

            @pl.when(main_ok)
            def _():
                act(halo(1))
                act(halo(2))

            @pl.when(edge_ok)
            def _():
                act(halo(3))
                act(halo(4))

    def arrive(slot, k):
        lo, hi = chunks[k]
        pltpu.make_async_remote_copy(
            src_ref=own.at[pl.ds(lo, hi - lo), pl.ds(0, half), :],
            dst_ref=buf.at[slot, pl.ds(lo, hi - lo)],
            send_sem=ssem.at[0, k],
            recv_sem=rsem.at[slot, k],
            device_id=at(q, 1 - c, t),
            device_id_type=MESH,
        ).wait_recv()

    def halo_wait(slot):
        @pl.when(t < nt - 1)
        def _():
            pltpu.make_async_remote_copy(
                src_ref=own.at[0, pl.ds(0, half), :],
                dst_ref=buf.at[slot, segs],
                send_sem=hsend.at[0],
                recv_sem=hrecv.at[slot],
                device_id=at(q, c, t + 1),
                device_id_type=MESH,
            ).wait_recv()

    def main_start(k):
        @pl.when(main_ok)
        def _():
            stream(1, k).start()
            stream(2, k).start()

    def main_left(k):
        @pl.when(main_ok)
        def _():
            stream(1, k).wait_send()
            stream(2, k).wait_send()

    def edge_start(k):
        @pl.when(edge_ok)
        def _():
            stream(3, k).start()
            stream(4, k).start()

    stream(0, 0).start()
    main_start(0)
    halos(lambda copy: copy.start())
    for k in range(1, steps):
        stream(0, k).start()
    main_start(1)

    @pl.when(c == 1)
    def _():
        for k in range(2, steps):
            main_start(k)

    for copy in tables:
        copy.wait()

    taper_rise, taper_fall = taper[0:1, :], taper[1:2, :]
    quarter = HOP // 2

    def whiten(parts):
        sums, differences = [], []
        for slot, first, count in parts:
            samples = buf[slot, first : first + count + 1].astype(F32)
            rise, fall = samples[:count] * taper_rise, samples[1:] * taper_fall
            sums.append((rise + fall).astype(BF16).reshape(count * half, HOP))
            differences.append((rise - fall).astype(BF16).reshape(count * half, HOP))
        even = jnp.dot(jnp.concatenate(sums, 0), fwd[0], preferred_element_type=F32)
        odd = jnp.dot(jnp.concatenate(differences, 0), fwd[1], preferred_element_type=F32)
        power = [
            (z[:, :quarter] * z[:, :quarter] + z[:, quarter:] * z[:, quarter:]).astype(BF16)
            for z in (even, odd)
        ]
        smooth = jnp.dot(jnp.concatenate(power, 1), band[...], preferred_element_type=F32)
        factor = lax.rsqrt(smooth + 1e-06)
        row = 0
        for slot, first, count in parts:
            rows = slice(row, row + count * half)
            row += count * half
            for n, z in enumerate((even, odd)):
                scale = factor[rows, n * quarter : (n + 1) * quarter]
                for m in range(2):
                    value = (z[rows, m * quarter : (m + 1) * quarter] * scale).astype(BF16)
                    lanes = slice(m * HOP + n * quarter, m * HOP + (n + 1) * quarter)
                    white[slot, first : first + count, :, lanes] = value.reshape(count, half, quarter)

    def cross(pairs, start, count):
        slots = []
        for _, first, second in pairs:
            for slot in (first, second):
                if not any(slot is s for s in slots):
                    slots.append(slot)

        def tile(i, carry):
            rows = pl.ds(pl.multiple_of(16 * (i // 4), 16), 16)
            lanes = pl.multiple_of(128 * lax.rem(i, 4), 128)
            lanes_re, lanes_im = pl.ds(lanes, 128), pl.ds(HOP + lanes, 128)
            sums = [[acc[p, rows, lanes_re], acc[p, rows, lanes_im]] for p, _, _ in pairs]
            for seg in range(start, start + count):
                values = [
                    (
                        white[slot, seg, rows, lanes_re].astype(F32),
                        white[slot, seg, rows, lanes_im].astype(F32),
                    )
                    for slot in slots
                ]
                for n, (_, first, second) in enumerate(pairs):
                    a_re, a_im = [v for s, v in zip(slots, values) if s is first][0]
                    b_re, b_im = [v for s, v in zip(slots, values) if s is second][0]
                    sums[n][0] += a_re * b_re + a_im * b_im
                    sums[n][1] += a_im * b_re - a_re * b_im
            for n, (p, _, _) in enumerate(pairs):
                acc[p, rows, lanes_re] = sums[n][0]
                acc[p, rows, lanes_im] = sums[n][1]
            return carry

        lax.fori_loop(0, (half // 16) * 4, tile, 0)

    def lags_of(first, count):
        stack = acc[first : first + count].reshape(count * half, NFFT)
        high = stack.astype(BF16)
        low = (stack - high.astype(F32)).astype(BF16)
        both = jnp.concatenate([high, low], 0)
        sides = []
        for n in range(2):
            lanes = slice(n * quarter, (n + 1) * quarter)
            lanes_im = slice(HOP + n * quarter, HOP + (n + 1) * quarter)
            side = jnp.dot(
                jnp.concatenate([both[:, lanes], both[:, lanes_im]], 1),
                lagt[n],
                preferred_element_type=F32,
            )
            sides.append(side[: count * half] + side[count * half :])
        even, odd = sides
        lags = jnp.concatenate([(even + odd).astype(BF16), (even - odd).astype(BF16)], 1)
        for time in range(nt):
            part[time, first : first + count] = lags[:, time * cols : (time + 1) * cols].reshape(
                count, half, cols
            )

    def exchange(group, first, count, d):
        peer = lax.rem(t + d, nt)
        return pltpu.make_async_remote_copy(
            src_ref=part.at[peer, pl.ds(first, count)],
            dst_ref=gath.at[t, pl.ds(first, count)],
            send_sem=asend.at[group, d],
            recv_sem=arecv.at[group, t],
            device_id=at(q, c, peer),
            device_id_type=MESH,
        )

    def collect(group, first, count):
        gath[t, first : first + count] = part[t, first : first + count]
        for d in range(1, nt):
            source = lax.rem(t + d, nt)
            pltpu.make_async_remote_copy(
                src_ref=part.at[source, pl.ds(first, count)],
                dst_ref=gath.at[source, pl.ds(first, count)],
                send_sem=asend.at[group, d],
                recv_sem=arecv.at[group, source],
                device_id=at(q, c, source),
                device_id_type=MESH,
            ).wait_recv()
        total = gath[0, first : first + count].astype(F32)
        for time in range(1, nt):
            total += gath[time, first : first + count].astype(F32)
        fin[first : first + count] = total

    def deliver(kind):
        if kind == 0:
            src, dst = fin.at[pl.ds(0, 3)], res.at[pl.ds(0, 3), pl.ds(half * c, half), :]
            device = at(q - 1, 1, t)
        elif kind == 1:
            src, dst = fin.at[pl.ds(3, 2)], res.at[pl.ds(0, 2), pl.ds(half * c, half), :]
            device = at(q, 0, t)
        else:
            src, dst = fin.at[pl.ds(5, 1)], res.at[pl.ds(2, 1), pl.ds(half * c, half), :]
            device = at(q, 0, t)
        return pltpu.make_async_remote_copy(
            src_ref=src,
            dst_ref=dst,
            send_sem=fsend.at[kind],
            recv_sem=frecv.at[kind, c],
            device_id=device,
            device_id_type=MESH,
        )

    def delivered(kind, core):
        first, count = ((0, 3), (3, 2), (5, 1))[kind]
        pltpu.make_async_remote_copy(
            src_ref=fin.at[pl.ds(first, count)],
            dst_ref=res.at[pl.ds(2 if kind == 2 else 0, count), pl.ds(half * core, half), :],
            send_sem=fsend.at[kind],
            recv_sem=frecv.at[kind, core],
            device_id=at(q, 1 - c, t),
            device_id_type=MESH,
        ).wait_recv()

    acc[...] = jnp.zeros(acc.shape, F32)

    whiten([(mine, 0, 8)])
    arrive(theirs, 0)
    halo_wait(mine)
    whiten([(mine, 8, 8)])
    arrive(theirs, 1)
    whiten([(theirs, 0, 8)])
    cross([(3, SLOT_B, SLOT_C)], 0, 8)
    arrive(theirs, 2)
    arrive(theirs, 3)

    def arrive_sides(k):
        @pl.when(below)
        def _():
            arrive(SLOT_A, k)

        @pl.when(above)
        def _():
            arrive(SLOT_D, k)

    halo_wait(theirs)
    whiten([(theirs, 8, 8)])
    cross([(3, SLOT_B, SLOT_C)], 8, 8)

    for k in range(steps):
        arrive_sides(k)

        @pl.when(c == 0)
        def _():
            main_left(k)
            if k + 2 < steps:
                main_start(k + 2)

        if k + 2 >= steps:
            edge_start(2 * (k + 2 - steps))
            edge_start(2 * (k + 2 - steps) + 1)
        if k == steps - 1:
            @pl.when(below)
            def _():
                halo_wait(SLOT_A)

            @pl.when(above)
            def _():
                halo_wait(SLOT_D)

        whiten([(SLOT_A, 4 * k, 4), (SLOT_D, 4 * k, 4)])
        cross(
            [(0, SLOT_A, SLOT_B), (1, SLOT_A, SLOT_C), (2, SLOT_A, SLOT_D), (4, SLOT_B, SLOT_D)],
            4 * k,
            4,
        )

    lags_of(0, 5)
    for d in range(1, nt):
        exchange(0, 0, 5, d).start()


    for k in range(steps):
        @pl.when(above)
        def _():
            arrive(SLOT_E, k)
            if k == steps - 1:
                halo_wait(SLOT_E)

        whiten([(SLOT_E, 4 * k, 4)])
        cross([(5, SLOT_B, SLOT_E)], 4 * k, 4)

    lags_of(5, 1)
    for d in range(1, nt):
        exchange(1, 5, 1, d).start()

    collect(0, 0, 5)

    @pl.when(below)
    def _():
        deliver(0).start()

    @pl.when(c == 1)
    def _():
        deliver(1).start()

    @pl.when(c == 0)
    def _():
        res[0:2, 0:half] = fin[3:5]

    collect(1, 5, 1)

    @pl.when(c == 1)
    def _():
        deliver(2).start()

    @pl.when(c == 0)
    def _():
        res[2, 0:half] = fin[5]
        delivered(1, 1)
        delivered(2, 1)

    @pl.when(jnp.logical_and(c == 1, above))
    def _():
        delivered(0, 0)
        delivered(0, 1)

    for slot in range(LIMIT):
        reach = partners[0, slot] - chan
        row = jnp.zeros((chans, cols), F32)
        for offset in range(LIMIT):
            row = jnp.where(reach == offset + 1, res[offset], row)
        out_ref[slot] = row

    for k in range(steps):
        stream(0, k).wait_send()

        @pl.when(c == 1)
        def _():
            main_left(k)

        @pl.when(edge_ok)
        def _():
            stream(3, k).wait_send()
            stream(4, k).wait_send()

    halos(lambda copy: copy.wait_send())

    for d in range(1, nt):
        exchange(0, 0, 5, d).wait_send()
        exchange(1, 5, 1, d).wait_send()

    @pl.when(below)
    def _():
        deliver(0).wait_send()

    @pl.when(c == 1)
    def _():
        deliver(1).wait_send()
        deliver(2).wait_send()


def solution(mesh):
    nq, nt = mesh.shape["chan"] // 2, mesh.shape["tm"]

    def per_device(traces, live_channels, partners):
        chans, samples = traces.shape
        half = chans // 2
        segs = samples // HOP
        steps = segs // 4
        cols = NFFT // nt
        anywhere = pl.BlockSpec(memory_space=pltpu.HBM)
        by_slot = pl.pallas_call(
            functools.partial(kernel, nq, nt, segs, chans),
            out_shape=jax.ShapeDtypeStruct((LIMIT, chans, cols), F32),
            in_specs=[anywhere] * 7,
            out_specs=pl.BlockSpec(memory_space=pltpu.VMEM),
            scratch_shapes=[
                pltpu.SMEM((1,), jnp.int32),
                pltpu.SMEM((1, LIMIT), jnp.int32),
                pltpu.VMEM((2, HOP), F32),
                pltpu.VMEM((segs, chans, HOP), BF16),
                pltpu.VMEM((5, segs + 1, half, HOP), BF16),
                pltpu.VMEM((5, segs, half, NFFT), BF16),
                pltpu.VMEM((PAIRS, half, NFFT), F32),
                pltpu.VMEM((2, HOP, HOP), BF16),
                pltpu.VMEM((HOP, HOP), BF16),
                pltpu.VMEM((2, HOP, HOP), BF16),
                pltpu.VMEM((nt, PAIRS, half, cols), BF16),
                pltpu.VMEM((nt, PAIRS, half, cols), BF16),
                pltpu.VMEM((PAIRS, half, cols), F32),
                pltpu.VMEM((LIMIT, chans, cols), F32),
                pltpu.SemaphoreType.DMA((segs,)),
                pltpu.SemaphoreType.DMA((6,)),
                pltpu.SemaphoreType.DMA((5, steps)),
                pltpu.SemaphoreType.DMA((5, steps)),
                pltpu.SemaphoreType.DMA((6,)),
                pltpu.SemaphoreType.DMA((5,)),
                pltpu.SemaphoreType.DMA((2, nt)),
                pltpu.SemaphoreType.DMA((2, nt)),
                pltpu.SemaphoreType.DMA((3,)),
                pltpu.SemaphoreType.DMA((3, 2)),
            ],
            compiler_params=pltpu.CompilerParams(
                collective_id=0, has_side_effects=True, vmem_limit_bytes=56 * 1024 * 1024
            ),
        )(
            live_channels,
            partners,
            traces,
            jnp.asarray(taper_rows()),
            jnp.asarray(forward_tables()),
            jnp.asarray(band_table()),
            jnp.asarray(lag_tables(segs * nt)),
        )
        return by_slot.transpose(1, 0, 2)

    in_specs = (P("chan", "tm"), P("chan"), P("chan", None))
    out_specs = P("chan", None, "tm")
    return jax.shard_map(
        per_device, mesh=mesh, in_specs=in_specs, out_specs=out_specs, check_vma=False
    )
```

time: 370 us -> 59.4 us (0.16)
  the two profiles are of different devices: /device:TPU:1 before, /device:TPU:477 now
where the time goes in v1:
time: 59.4 us; the launch traced here: 59.2 us
  Pallas kernels  57 us (96%)
  local copies, waits for them, and re-layouts  1.58 us (3%)
  between operations  0.66 us (1%)
    pallas_call x1, Pallas kernels, per_device(): pl.pallas_call(functools.partial(kernel, nq, nt, segs, chans), out_shape=...  57 us
    unnamed x1, local copies, waits for them, and re-layouts  1.58 us

profile of v1, /device:TPU:477, one launch (start us, length us, event | category | flops | bytes accessed | tf_op | source)
XLA Modules:
  0.0 59.2 jit_solution(7386356772276200382)
XLA Ops:
  0.7 57.0 %shard_map.73 = f32[3,96,128]{2,1,0:T(8,128)} custom-call(s32[1]{0:T(128)S(6)} %copy.9.live_hbm, s32[1,3]{1,0:T(1,128)} %partners_hbm.1, bf16[96,8192]{1,0:T(8,128)(2,1)} %x_ref.1, f32[2,512]{1,0:T(2,128)} %constant.8.clone.taper_hbm, bf16[2,512,512]{2,1,0:T(8,128)(2,1)} %constant.9.clone.fwd_hbm, bf16[512,512]{1,0:T(8,128)(2,1)} %constant.10.clone.band_hbm, ...), custom_call_target="tpu_custom_call" | custom-call | tf_op jit(solution)/shard_map/pallas_call | solution.py:563
  57.6 1.6 %copy.10 = f32[96,3,128]{2,0,1:T(8,128)} copy(f32[96,3,128]{2,0,1:T(8,128)} %bitcast.1) | data formatting | bytes 294912

commit v2 on v1

--- a/solution.py
+++ b/solution.py
@@ -18,8 +18,8 @@
 F32 = jnp.float32
 BF16 = jnp.bfloat16
 
-SLOT_A, SLOT_B, SLOT_C, SLOT_D, SLOT_E = range(5)
-PAIRS = 6
+SLOT_A, SLOT_B, SLOT_C, SLOT_D, SLOT_E, SLOT_G = range(6)
+PAIRS = 9
 
 
 def bin_order():
@@ -79,6 +79,9 @@
     q = chan // 2
     c = lax.rem(chan, 2)
     below, above = q > 0, q < nq - 1
+    corner = q == nq - 2
+    from_below = jnp.logical_and(q > 0, q < nq - 1)
+    incoming = jnp.logical_and(q < nq - 1, c + q > 0)
     mine = SLOT_B + c
     theirs = SLOT_C - c
 
@@ -99,19 +102,25 @@
     for copy in tables:
         copy.start()
 
-    @pl.when(q == 0)
+    @pl.when(jnp.logical_not(from_below))
     def _():
         buf[SLOT_A] = jnp.zeros((segs + 1, half, HOP), BF16)
 
     @pl.when(q == nq - 1)
     def _():
         buf[SLOT_D] = jnp.zeros((segs + 1, half, HOP), BF16)
+
+    @pl.when(q >= nq - 2)
+    def _():
+        res[...] = jnp.zeros(res.shape, F32)
+
+    @pl.when(jnp.logical_not(incoming))
+    def _():
         buf[SLOT_E] = jnp.zeros((segs + 1, half, HOP), BF16)
-        res[...] = jnp.zeros(res.shape, F32)
 
     @pl.when(t == nt - 1)
     def _():
-        for slot in range(5):
+        for slot in range(6):
             buf[slot, segs] = jnp.zeros((half, HOP), BF16)
 
     barrier = pltpu.get_barrier_semaphore()
@@ -164,16 +173,19 @@
     pl.semaphore_wait(barrier, nt - 1 + around * times)
 
     outward = 2 * c - 1
-    main_ok = jnp.where(c == 0, q, nq - 1 - q) > 0
-    edge_ok = c * q > 0
+    main_ok = jnp.where(c == 0, q, nq - 2 - q) > 0
+    edge_ok = jnp.where(c == 0, nq - 2 - q, q) > 0
+    extra_ok = jnp.logical_and(c == 1, q == nq - 1)
 
     def route(index):
         if index == 0:
             return half * (1 - c), mine, q, 1 - c
         if index in (1, 2):
             return half * (index - 1), 3 * (1 - c), q + outward, index - 1
-        if index in (3, 4):
-            return half * (index - 3), SLOT_E, q - 1, index - 3
+        if index == 3:
+            return half * c, SLOT_E, q - outward, c
+        if index == 5:
+            return 0, SLOT_G, q - 1, 0
         return half * c, mine, q, c
 
     def stream(index, k):
@@ -202,7 +214,7 @@
     def halos(act):
         @pl.when(t > 0)
         def _():
-            act(halo(5))
+            act(halo(4))
             act(halo(0))
 
             @pl.when(main_ok)
@@ -213,7 +225,10 @@
             @pl.when(edge_ok)
             def _():
                 act(halo(3))
-                act(halo(4))
+
+            @pl.when(extra_ok)
+            def _():
+                act(halo(5))
 
     def arrive(slot, k):
         lo, hi = chunks[k]
@@ -254,7 +269,10 @@
         @pl.when(edge_ok)
         def _():
             stream(3, k).start()
-            stream(4, k).start()
+
+        @pl.when(extra_ok)
+        def _():
+            stream(5, k).start()
 
     stream(0, 0).start()
     main_start(0)
@@ -262,11 +280,6 @@
     for k in range(1, steps):
         stream(0, k).start()
     main_start(1)
-
-    @pl.when(c == 1)
-    def _():
-        for k in range(2, steps):
-            main_start(k)
 
     for copy in tables:
         copy.wait()
@@ -386,12 +399,15 @@
         if kind == 0:
             src, dst = fin.at[pl.ds(0, 3)], res.at[pl.ds(0, 3), pl.ds(half * c, half), :]
             device = at(q - 1, 1, t)
+        elif kind == 3:
+            src, dst = fin.at[pl.ds(6, 2)], res.at[pl.ds(0, 2), pl.ds(0, half), :]
+            device = at(q, 1, t)
         elif kind == 1:
             src, dst = fin.at[pl.ds(3, 2)], res.at[pl.ds(0, 2), pl.ds(half * c, half), :]
             device = at(q, 0, t)
         else:
             src, dst = fin.at[pl.ds(5, 1)], res.at[pl.ds(2, 1), pl.ds(half * c, half), :]
-            device = at(q, 0, t)
+            device = at(jnp.where(c == 0, q - 1, q), 0, t)
         return pltpu.make_async_remote_copy(
             src_ref=src,
             dst_ref=dst,
@@ -402,7 +418,7 @@
         )
 
     def delivered(kind, core):
-        first, count = ((0, 3), (3, 2), (5, 1))[kind]
+        first, count = ((0, 3), (3, 2), (5, 1), (6, 2))[kind]
         pltpu.make_async_remote_copy(
             src_ref=fin.at[pl.ds(first, count)],
             dst_ref=res.at[pl.ds(2 if kind == 2 else 0, count), pl.ds(half * core, half), :],
@@ -425,7 +441,7 @@
     arrive(theirs, 3)
 
     def arrive_sides(k):
-        @pl.when(below)
+        @pl.when(from_below)
         def _():
             arrive(SLOT_A, k)
 
@@ -438,19 +454,15 @@
     cross([(3, SLOT_B, SLOT_C)], 8, 8)
 
     for k in range(steps):
-        arrive_sides(k)
-
-        @pl.when(c == 0)
-        def _():
-            main_left(k)
-            if k + 2 < steps:
-                main_start(k + 2)
-
-        if k + 2 >= steps:
+        main_left(k)
+        if k + 2 < steps:
+            main_start(k + 2)
+        else:
             edge_start(2 * (k + 2 - steps))
             edge_start(2 * (k + 2 - steps) + 1)
+        arrive_sides(k)
         if k == steps - 1:
-            @pl.when(below)
+            @pl.when(from_below)
             def _():
                 halo_wait(SLOT_A)
 
@@ -469,24 +481,45 @@
     for d in range(1, nt):
         exchange(0, 0, 5, d).start()
 
+    first_white = jnp.where(c == 0, SLOT_E, SLOT_B)
+    second_white = jnp.where(c == 0, SLOT_C, SLOT_E)
 
     for k in range(steps):
-        @pl.when(above)
+        @pl.when(incoming)
         def _():
             arrive(SLOT_E, k)
             if k == steps - 1:
                 halo_wait(SLOT_E)
 
         whiten([(SLOT_E, 4 * k, 4)])
-        cross([(5, SLOT_B, SLOT_E)], 4 * k, 4)
+        cross([(5, first_white, second_white)], 4 * k, 4)
 
     lags_of(5, 1)
     for d in range(1, nt):
         exchange(1, 5, 1, d).start()
 
+    second = jnp.where(c == 0, SLOT_G, SLOT_E)
+
+    @pl.when(corner)
+    def _():
+        @pl.when(c == 0)
+        def _():
+            for k in range(steps):
+                arrive(SLOT_G, k)
+            halo_wait(SLOT_G)
+            whiten([(SLOT_G, 0, 8)])
+            whiten([(SLOT_G, 8, 8)])
+
+        pairs = [(6, SLOT_C, SLOT_D), (7, SLOT_C, second), (8, SLOT_B, second)]
+        cross(pairs, 0, 8)
+        cross(pairs, 8, 8)
+        lags_of(6, 3)
+        for d in range(1, nt):
+            exchange(2, 6, 3, d).start()
+
     collect(0, 0, 5)
 
-    @pl.when(below)
+    @pl.when(from_below)
     def _():
         deliver(0).start()
 
@@ -499,21 +532,41 @@
         res[0:2, 0:half] = fin[3:5]
 
     collect(1, 5, 1)
-
-    @pl.when(c == 1)
+    last_ok = jnp.logical_or(c == 1, from_below)
+
+    @pl.when(last_ok)
     def _():
         deliver(2).start()
 
+    @pl.when(corner)
+    def _():
+        collect(2, 6, 3)
+
+        @pl.when(c == 0)
+        def _():
+            deliver(3).start()
+            res[2, 0:half] = fin[8]
+
+        @pl.when(c == 1)
+        def _():
+            res[0:2, half:chans] = fin[6:8]
+            delivered(3, 0)
+
     @pl.when(c == 0)
     def _():
-        res[2, 0:half] = fin[5]
         delivered(1, 1)
         delivered(2, 1)
 
-    @pl.when(jnp.logical_and(c == 1, above))
-    def _():
-        delivered(0, 0)
-        delivered(0, 1)
+    @pl.when(q < nq - 2)
+    def _():
+        @pl.when(c == 0)
+        def _():
+            delivered(2, 0)
+
+        @pl.when(c == 1)
+        def _():
+            delivered(0, 0)
+            delivered(0, 1)
 
     for slot in range(LIMIT):
         reach = partners[0, slot] - chan
@@ -525,14 +578,13 @@
     for k in range(steps):
         stream(0, k).wait_send()
 
-        @pl.when(c == 1)
-        def _():
-            main_left(k)
-
         @pl.when(edge_ok)
         def _():
             stream(3, k).wait_send()
-            stream(4, k).wait_send()
+
+        @pl.when(extra_ok)
+        def _():
+            stream(5, k).wait_send()
 
     halos(lambda copy: copy.wait_send())
 
@@ -540,13 +592,25 @@
         exchange(0, 0, 5, d).wait_send()
         exchange(1, 5, 1, d).wait_send()
 
-    @pl.when(below)
+    @pl.when(corner)
+    def _():
+        for d in range(1, nt):
+            exchange(2, 6, 3, d).wait_send()
+
+        @pl.when(c == 0)
+        def _():
+            deliver(3).wait_send()
+
+    @pl.when(from_below)
     def _():
         deliver(0).wait_send()
 
     @pl.when(c == 1)
     def _():
         deliver(1).wait_send()
+
+    @pl.when(last_ok)
+    def _():
         deliver(2).wait_send()
 
 
@@ -570,8 +634,8 @@
                 pltpu.SMEM((1, LIMIT), jnp.int32),
                 pltpu.VMEM((2, HOP), F32),
                 pltpu.VMEM((segs, chans, HOP), BF16),
-                pltpu.VMEM((5, segs + 1, half, HOP), BF16),
-                pltpu.VMEM((5, segs, half, NFFT), BF16),
+                pltpu.VMEM((6, segs + 1, half, HOP), BF16),
+                pltpu.VMEM((6, segs, half, NFFT), BF16),
                 pltpu.VMEM((PAIRS, half, NFFT), F32),
                 pltpu.VMEM((2, HOP, HOP), BF16),
                 pltpu.VMEM((HOP, HOP), BF16),
@@ -582,14 +646,14 @@
                 pltpu.VMEM((LIMIT, chans, cols), F32),
                 pltpu.SemaphoreType.DMA((segs,)),
                 pltpu.SemaphoreType.DMA((6,)),
-                pltpu.SemaphoreType.DMA((5, steps)),
-                pltpu.SemaphoreType.DMA((5, steps)),
+                pltpu.SemaphoreType.DMA((6, steps)),
+                pltpu.SemaphoreType.DMA((6, steps)),
                 pltpu.SemaphoreType.DMA((6,)),
-                pltpu.SemaphoreType.DMA((5,)),
-                pltpu.SemaphoreType.DMA((2, nt)),
-                pltpu.SemaphoreType.DMA((2, nt)),
-                pltpu.SemaphoreType.DMA((3,)),
-                pltpu.SemaphoreType.DMA((3, 2)),
+                pltpu.SemaphoreType.DMA((6,)),
+                pltpu.SemaphoreType.DMA((3, nt)),
+                pltpu.SemaphoreType.DMA((3, nt)),
+                pltpu.SemaphoreType.DMA((4,)),
+                pltpu.SemaphoreType.DMA((4, 2)),
             ],
             compiler_params=pltpu.CompilerParams(
                 collective_id=0, has_side_effects=True, vmem_limit_bytes=56 * 1024 * 1024

time: 59.4 us -> 57.2 us (0.963)
  the two profiles are of different devices: /device:TPU:477 before, /device:TPU:453 now
where the time goes in v2:
time: 57.2 us; the launch traced here: 57 us
  Pallas kernels  54.8 us (96%)
  local copies, waits for them, and re-layouts  1.58 us (3%)
  between operations  0.66 us (1%)
    pallas_call x1, Pallas kernels, per_device(): pl.pallas_call(functools.partial(kernel, nq, nt, segs, chans), out_shape=...  54.8 us
    unnamed x1, local copies, waits for them, and re-layouts  1.58 us

profile of v2, /device:TPU:453, one launch (start us, length us, event | category | flops | bytes accessed | tf_op | source)
XLA Modules:
  0.0 57.0 jit_solution(10904495183674553653)
XLA Ops:
  0.7 54.8 %shard_map.73 = f32[3,96,128]{2,1,0:T(8,128)} custom-call(s32[1]{0:T(128)S(6)} %copy.9.live_hbm, s32[1,3]{1,0:T(1,128)} %partners_hbm.1, bf16[96,8192]{1,0:T(8,128)(2,1)} %x_ref.1, f32[2,512]{1,0:T(2,128)} %constant.8.clone.taper_hbm, bf16[2,512,512]{2,1,0:T(8,128)(2,1)} %constant.9.clone.fwd_hbm, bf16[512,512]{1,0:T(8,128)(2,1)} %constant.10.clone.band_hbm, ...), custom_call_target="tpu_custom_call" | custom-call | tf_op jit(solution)/shard_map/pallas_call | solution.py:627
  55.4 1.6 %copy.10 = f32[96,3,128]{2,0,1:T(8,128)} copy(f32[96,3,128]{2,0,1:T(8,128)} %bitcast.1) | data formatting | bytes 294912

commit v3 on v1

--- a/solution.py
+++ b/solution.py
@@ -19,7 +19,7 @@
 BF16 = jnp.bfloat16
 
 SLOT_A, SLOT_B, SLOT_C, SLOT_D, SLOT_E = range(5)
-PAIRS = 6
+PAIRS = 8
 
 
 def bin_order():
@@ -79,6 +79,9 @@
     q = chan // 2
     c = lax.rem(chan, 2)
     below, above = q > 0, q < nq - 1
+    corner = jnp.logical_and(q == nq - 2, c == 1)
+    from_below = jnp.logical_and(q > 0, q + c < nq)
+    incoming = jnp.where(c == 0, q, nq - 1 - q) > 0
     mine = SLOT_B + c
     theirs = SLOT_C - c
 
@@ -99,15 +102,21 @@
     for copy in tables:
         copy.start()
 
-    @pl.when(q == 0)
+    @pl.when(jnp.logical_not(from_below))
     def _():
         buf[SLOT_A] = jnp.zeros((segs + 1, half, HOP), BF16)
 
     @pl.when(q == nq - 1)
     def _():
         buf[SLOT_D] = jnp.zeros((segs + 1, half, HOP), BF16)
+
+    @pl.when(q >= nq - 2)
+    def _():
+        res[...] = jnp.zeros(res.shape, F32)
+
+    @pl.when(jnp.logical_not(incoming))
+    def _():
         buf[SLOT_E] = jnp.zeros((segs + 1, half, HOP), BF16)
-        res[...] = jnp.zeros(res.shape, F32)
 
     @pl.when(t == nt - 1)
     def _():
@@ -164,16 +173,16 @@
     pl.semaphore_wait(barrier, nt - 1 + around * times)
 
     outward = 2 * c - 1
-    main_ok = jnp.where(c == 0, q, nq - 1 - q) > 0
-    edge_ok = c * q > 0
+    main_ok = (jnp.where(c == 0, q, nq - 1 - q) > 0, jnp.where(c == 0, q, nq - 2 - q) > 0)
+    edge_ok = jnp.where(c == 0, nq - 1 - q, q) > 0
 
     def route(index):
         if index == 0:
             return half * (1 - c), mine, q, 1 - c
         if index in (1, 2):
             return half * (index - 1), 3 * (1 - c), q + outward, index - 1
-        if index in (3, 4):
-            return half * (index - 3), SLOT_E, q - 1, index - 3
+        if index == 3:
+            return half * c, SLOT_E, q - outward, c
         return half * c, mine, q, c
 
     def stream(index, k):
@@ -202,18 +211,17 @@
     def halos(act):
         @pl.when(t > 0)
         def _():
-            act(halo(5))
+            act(halo(4))
             act(halo(0))
 
-            @pl.when(main_ok)
-            def _():
-                act(halo(1))
-                act(halo(2))
+            for n in range(2):
+                @pl.when(main_ok[n])
+                def _():
+                    act(halo(1 + n))
 
             @pl.when(edge_ok)
             def _():
                 act(halo(3))
-                act(halo(4))
 
     def arrive(slot, k):
         lo, hi = chunks[k]
@@ -239,22 +247,21 @@
             ).wait_recv()
 
     def main_start(k):
-        @pl.when(main_ok)
-        def _():
-            stream(1, k).start()
-            stream(2, k).start()
+        for n in range(2):
+            @pl.when(main_ok[n])
+            def _():
+                stream(1 + n, k).start()
 
     def main_left(k):
-        @pl.when(main_ok)
-        def _():
-            stream(1, k).wait_send()
-            stream(2, k).wait_send()
+        for n in range(2):
+            @pl.when(main_ok[n])
+            def _():
+                stream(1 + n, k).wait_send()
 
     def edge_start(k):
         @pl.when(edge_ok)
         def _():
             stream(3, k).start()
-            stream(4, k).start()
 
     stream(0, 0).start()
     main_start(0)
@@ -262,11 +269,6 @@
     for k in range(1, steps):
         stream(0, k).start()
     main_start(1)
-
-    @pl.when(c == 1)
-    def _():
-        for k in range(2, steps):
-            main_start(k)
 
     for copy in tables:
         copy.wait()
@@ -391,7 +393,7 @@
             device = at(q, 0, t)
         else:
             src, dst = fin.at[pl.ds(5, 1)], res.at[pl.ds(2, 1), pl.ds(half * c, half), :]
-            device = at(q, 0, t)
+            device = at(jnp.where(c == 0, q - 1, q), 0, t)
         return pltpu.make_async_remote_copy(
             src_ref=src,
             dst_ref=dst,
@@ -418,6 +420,7 @@
     arrive(theirs, 0)
     halo_wait(mine)
     whiten([(mine, 8, 8)])
+    main_start(2)
     arrive(theirs, 1)
     whiten([(theirs, 0, 8)])
     cross([(3, SLOT_B, SLOT_C)], 0, 8)
@@ -425,7 +428,7 @@
     arrive(theirs, 3)
 
     def arrive_sides(k):
-        @pl.when(below)
+        @pl.when(from_below)
         def _():
             arrive(SLOT_A, k)
 
@@ -438,19 +441,16 @@
     cross([(3, SLOT_B, SLOT_C)], 8, 8)
 
     for k in range(steps):
+        main_left(k)
+        if k + 3 < steps:
+            main_start(k + 3)
+        else:
+            edge_start(k + 3 - steps)
+        if k == steps - 1:
+            edge_start(steps - 1)
         arrive_sides(k)
-
-        @pl.when(c == 0)
-        def _():
-            main_left(k)
-            if k + 2 < steps:
-                main_start(k + 2)
-
-        if k + 2 >= steps:
-            edge_start(2 * (k + 2 - steps))
-            edge_start(2 * (k + 2 - steps) + 1)
         if k == steps - 1:
-            @pl.when(below)
+            @pl.when(from_below)
             def _():
                 halo_wait(SLOT_A)
 
@@ -469,24 +469,35 @@
     for d in range(1, nt):
         exchange(0, 0, 5, d).start()
 
+    first_white = jnp.where(c == 0, SLOT_E, SLOT_B)
+    second_white = jnp.where(c == 0, SLOT_C, SLOT_E)
 
     for k in range(steps):
-        @pl.when(above)
+        @pl.when(incoming)
         def _():
             arrive(SLOT_E, k)
             if k == steps - 1:
                 halo_wait(SLOT_E)
 
         whiten([(SLOT_E, 4 * k, 4)])
-        cross([(5, SLOT_B, SLOT_E)], 4 * k, 4)
+        cross([(5, first_white, second_white)], 4 * k, 4)
 
     lags_of(5, 1)
     for d in range(1, nt):
         exchange(1, 5, 1, d).start()
 
+    @pl.when(corner)
+    def _():
+        pairs = [(6, SLOT_C, SLOT_D), (7, SLOT_C, SLOT_E)]
+        cross(pairs, 0, 8)
+        cross(pairs, 8, 8)
+        lags_of(6, 2)
+        for d in range(1, nt):
+            exchange(2, 6, 2, d).start()
+
     collect(0, 0, 5)
 
-    @pl.when(below)
+    @pl.when(from_below)
     def _():
         deliver(0).start()
 
@@ -499,20 +510,32 @@
         res[0:2, 0:half] = fin[3:5]
 
     collect(1, 5, 1)
-
-    @pl.when(c == 1)
+    last_ok = jnp.logical_or(c == 1, from_below)
+
+    @pl.when(last_ok)
     def _():
         deliver(2).start()
 
+    @pl.when(corner)
+    def _():
+        collect(2, 6, 2)
+        res[0:2, half:chans] = fin[6:8]
+
     @pl.when(c == 0)
     def _():
-        res[2, 0:half] = fin[5]
         delivered(1, 1)
         delivered(2, 1)
 
+        @pl.when(above)
+        def _():
+            delivered(2, 0)
+
     @pl.when(jnp.logical_and(c == 1, above))
     def _():
         delivered(0, 0)
+
+    @pl.when(jnp.logical_and(c == 1, q < nq - 2))
+    def _():
         delivered(0, 1)
 
     for slot in range(LIMIT):
@@ -525,14 +548,9 @@
     for k in range(steps):
         stream(0, k).wait_send()
 
-        @pl.when(c == 1)
-        def _():
-            main_left(k)
-
         @pl.when(edge_ok)
         def _():
             stream(3, k).wait_send()
-            stream(4, k).wait_send()
 
     halos(lambda copy: copy.wait_send())
 
@@ -540,13 +558,21 @@
         exchange(0, 0, 5, d).wait_send()
         exchange(1, 5, 1, d).wait_send()
 
-    @pl.when(below)
+    @pl.when(corner)
+    def _():
+        for d in range(1, nt):
+            exchange(2, 6, 2, d).wait_send()
+
+    @pl.when(from_below)
     def _():
         deliver(0).wait_send()
 
     @pl.when(c == 1)
     def _():
         deliver(1).wait_send()
+
+    @pl.when(last_ok)
+    def _():
         deliver(2).wait_send()
 
 
@@ -582,12 +608,12 @@
                 pltpu.VMEM((LIMIT, chans, cols), F32),
                 pltpu.SemaphoreType.DMA((segs,)),
                 pltpu.SemaphoreType.DMA((6,)),
+                pltpu.SemaphoreType.DMA((4, steps)),
                 pltpu.SemaphoreType.DMA((5, steps)),
-                pltpu.SemaphoreType.DMA((5, steps)),
-                pltpu.SemaphoreType.DMA((6,)),
                 pltpu.SemaphoreType.DMA((5,)),
-                pltpu.SemaphoreType.DMA((2, nt)),
-                pltpu.SemaphoreType.DMA((2, nt)),
+                pltpu.SemaphoreType.DMA((5,)),
+                pltpu.SemaphoreType.DMA((3, nt)),
+                pltpu.SemaphoreType.DMA((3, nt)),
                 pltpu.SemaphoreType.DMA((3,)),
                 pltpu.SemaphoreType.DMA((3, 2)),
             ],

time: 59.4 us -> 55.9 us (0.941)
  the two profiles are of different devices: /device:TPU:477 before, /device:TPU:1 now
where the time goes in v3:
time: 55.9 us; the launch traced here: 55.1 us
  Pallas kernels  52.8 us (94%)
  local copies, waits for them, and re-layouts  1.58 us (3%)
  between operations  0.66 us (1%)
    pallas_call x1, Pallas kernels, per_device(): pl.pallas_call(functools.partial(kernel, nq, nt, segs, chans), out_shape=...  52.8 us
    unnamed x1, local copies, waits for them, and re-layouts  1.58 us

profile of v3, /device:TPU:1, one launch (start us, length us, event | category | flops | bytes accessed | tf_op | source)
XLA Modules:
  0.0 55.1 jit_solution(625734156066721906)
XLA Ops:
  0.7 52.8 %shard_map.73 = f32[3,96,128]{2,1,0:T(8,128)} custom-call(s32[1]{0:T(128)S(6)} %copy.9.live_hbm, s32[1,3]{1,0:T(1,128)} %partners_hbm.1, bf16[96,8192]{1,0:T(8,128)(2,1)} %x_ref.1, f32[2,512]{1,0:T(2,128)} %constant.8.clone.taper_hbm, bf16[2,512,512]{2,1,0:T(8,128)(2,1)} %constant.9.clone.fwd_hbm, bf16[512,512]{1,0:T(8,128)(2,1)} %constant.10.clone.band_hbm, ...), custom_call_target="tpu_custom_call" | custom-call | tf_op jit(solution)/shard_map/pallas_call | solution.py:589
  53.5 1.6 %copy.10 = f32[96,3,128]{2,0,1:T(8,128)} copy(f32[96,3,128]{2,0,1:T(8,128)} %bitcast.1) | data formatting | bytes 294912

commit v4 on v3

--- a/solution.py
+++ b/solution.py
@@ -166,7 +166,7 @@
         buf[mine, h] = own[h, pl.ds(pl.multiple_of(half * c, half), half), :]
         return carry
 
-    lax.fori_loop(0, segs, mask_one, 0)
+    lax.fori_loop(0, chunks[0][1], mask_one, 0)
 
     around = 1 + 2 * jnp.where(below, 1, 0) + 2 * jnp.where(above, 1, 0)
     times = 1 + jnp.where(t > 0, 1, 0) + jnp.where(t < nt - 1, 1, 0)
@@ -266,6 +266,7 @@
     stream(0, 0).start()
     main_start(0)
     halos(lambda copy: copy.start())
+    lax.fori_loop(chunks[0][1], segs, mask_one, 0)
     for k in range(1, steps):
         stream(0, k).start()
     main_start(1)
@@ -420,7 +421,6 @@
     arrive(theirs, 0)
     halo_wait(mine)
     whiten([(mine, 8, 8)])
-    main_start(2)
     arrive(theirs, 1)
     whiten([(theirs, 0, 8)])
     cross([(3, SLOT_B, SLOT_C)], 0, 8)
@@ -442,12 +442,11 @@
 
     for k in range(steps):
         main_left(k)
-        if k + 3 < steps:
-            main_start(k + 3)
+        if k + 2 < steps:
+            main_start(k + 2)
         else:
-            edge_start(k + 3 - steps)
-        if k == steps - 1:
-            edge_start(steps - 1)
+            edge_start(2 * (k + 2 - steps))
+            edge_start(2 * (k + 2 - steps) + 1)
         arrive_sides(k)
         if k == steps - 1:
             @pl.when(from_below)
@@ -472,15 +471,16 @@
     first_white = jnp.where(c == 0, SLOT_E, SLOT_B)
     second_white = jnp.where(c == 0, SLOT_C, SLOT_E)
 
-    for k in range(steps):
+    for chunks_in, first, count in (((0, 1), 0, 8), ((2,), 8, 4), ((3,), 12, 4)):
         @pl.when(incoming)
         def _():
-            arrive(SLOT_E, k)
-            if k == steps - 1:
+            for k in chunks_in:
+                arrive(SLOT_E, k)
+            if first + count == segs:
                 halo_wait(SLOT_E)
 
-        whiten([(SLOT_E, 4 * k, 4)])
-        cross([(5, first_white, second_white)], 4 * k, 4)
+        whiten([(SLOT_E, first, count)])
+        cross([(5, first_white, second_white)], first, count)
 
     lags_of(5, 1)
     for d in range(1, nt):
@@ -629,7 +629,8 @@
             jnp.asarray(band_table()),
             jnp.asarray(lag_tables(segs * nt)),
         )
-        return by_slot.transpose(1, 0, 2)
+        alive = jnp.arange(chans, dtype=jnp.int32)[:, None, None] < live_channels.reshape(1, 1, 1)
+        return jnp.where(alive, by_slot.transpose(1, 0, 2), F32(0.0))
 
     in_specs = (P("chan", "tm"), P("chan"), P("chan", None))
     out_specs = P("chan", None, "tm")

time: 55.9 us -> 55.2 us (0.987); the launches traced: 55.1 us -> 55.1 us
  other arithmetic: 0 us -> 1.66 us
  local copies, waits for them, and re-layouts: 1.58 us -> 0 us
    select_n x0 -> x1, other arithmetic: none -> 1.65 us  [per_device(): return jnp.where(alive, by_slot.transpose(1, 0, 2), F32(0.0))]
    unnamed x1 -> x0, local copies, waits for them, and re-layouts: 1.58 us -> none
where the time goes in v4:
time: 55.2 us; the launch traced here: 55.1 us
  Pallas kernels  52.8 us (96%)
  other arithmetic  1.66 us (3%)
  between operations  0.67 us (1%)
    pallas_call x1, Pallas kernels, per_device(): pl.pallas_call(functools.partial(kernel, nq, nt, segs, chans), out_shape=...  52.8 us
    select_n x1, other arithmetic, per_device(): return jnp.where(alive, by_slot.transpose(1, 0, 2), F32(0.0))  1.65 us

profile of v4, /device:TPU:1, one launch (start us, length us, event | category | flops | bytes accessed | tf_op | source)
XLA Modules:
  0.0 55.1 jit_solution(10255314826401868492)
XLA Ops:
  0.7 52.8 %shard_map.73 = f32[3,96,128]{2,1,0:T(8,128)} custom-call(s32[1]{0:T(128)} %copy.8.live_hbm, s32[1,3]{1,0:T(1,128)} %partners_hbm.1, bf16[96,8192]{1,0:T(8,128)(2,1)} %x_ref.1, f32[2,512]{1,0:T(2,128)} %constant.10.clone.taper_hbm, bf16[2,512,512]{2,1,0:T(8,128)(2,1)} %constant.11.clone.fwd_hbm, bf16[512,512]{1,0:T(8,128)(2,1)} %constant.12.clone.band_hbm, ...), custom_call_target="tpu_custom_call" | custom-call | tf_op jit(solution)/shard_map/pallas_call | solution.py:589
  53.4 1.7 %select_bitcast_fusion = f32[96,3,128]{2,0,1:T(8,128)} fusion(f32[3,96,128]{2,1,0:T(8,128)} %shard_map.73, pred[96]{0:T(512)(128)(4,1)S(1)} %iota_compare_fusion), kind=kLoop, calls=%fused_computation | loop fusion | flops 36864 | bytes 295008 | tf_op jit(solution)/shard_map/jit(_where)/select_n | solution.py:633
  (1 shorter events, 0.0 us)

commit v5 on v4

--- a/solution.py
+++ b/solution.py
@@ -88,8 +88,52 @@
     def at(chip, core, time):
         return {"chan": 2 * chip + core, "tm": time}
 
-    for h in range(segs):
+    def load(h):
         pltpu.make_async_copy(x_ref.at[:, pl.ds(HOP * h, HOP)], own.at[h], load_sem.at[h]).start()
+
+    live_copy = pltpu.make_async_copy(live_hbm, live, table_sem.at[5])
+    live_copy.start()
+    for h in range(chunks[0][1]):
+        load(h)
+
+    @pl.when(q >= nq - 2)
+    def _():
+        res[...] = jnp.zeros(res.shape, F32)
+
+    barrier = pltpu.get_barrier_semaphore()
+
+    def greet(chip, core, time):
+        pl.semaphore_signal(barrier, inc=1, device_id=at(chip, core, time), device_id_type=MESH)
+
+    for d in range(1, nt):
+        greet(q, c, lax.rem(t + d, nt))
+
+    def greet_around(time):
+        greet(q, 1 - c, time)
+
+        @pl.when(below)
+        def _():
+            greet(q - 1, 0, time)
+            greet(q - 1, 1, time)
+
+        @pl.when(above)
+        def _():
+            greet(q + 1, 0, time)
+            greet(q + 1, 1, time)
+
+    greet_around(t)
+
+    @pl.when(t > 0)
+    def _():
+        greet_around(t - 1)
+
+    @pl.when(t < nt - 1)
+    def _():
+        greet_around(t + 1)
+
+    for h in range(chunks[0][1], segs):
+        load(h)
+
     tables = [
         pltpu.make_async_copy(fwd_hbm, fwd, table_sem.at[0]),
         pltpu.make_async_copy(band_hbm, band, table_sem.at[1]),
@@ -97,8 +141,6 @@
         pltpu.make_async_copy(taper_hbm, taper, table_sem.at[3]),
         pltpu.make_async_copy(partners_hbm, partners, table_sem.at[4]),
     ]
-    live_copy = pltpu.make_async_copy(live_hbm, live, table_sem.at[5])
-    live_copy.start()
     for copy in tables:
         copy.start()
 
@@ -110,10 +152,6 @@
     def _():
         buf[SLOT_D] = jnp.zeros((segs + 1, half, HOP), BF16)
 
-    @pl.when(q >= nq - 2)
-    def _():
-        res[...] = jnp.zeros(res.shape, F32)
-
     @pl.when(jnp.logical_not(incoming))
     def _():
         buf[SLOT_E] = jnp.zeros((segs + 1, half, HOP), BF16)
@@ -122,37 +160,6 @@
     def _():
         for slot in range(5):
             buf[slot, segs] = jnp.zeros((half, HOP), BF16)
-
-    barrier = pltpu.get_barrier_semaphore()
-
-    def greet(chip, core, time):
-        pl.semaphore_signal(barrier, inc=1, device_id=at(chip, core, time), device_id_type=MESH)
-
-    for d in range(1, nt):
-        greet(q, c, lax.rem(t + d, nt))
-
-    def greet_around(time):
-        greet(q, 1 - c, time)
-
-        @pl.when(below)
-        def _():
-            greet(q - 1, 0, time)
-            greet(q - 1, 1, time)
-
-        @pl.when(above)
-        def _():
-            greet(q + 1, 0, time)
-            greet(q + 1, 1, time)
-
-    greet_around(t)
-
-    @pl.when(t > 0)
-    def _():
-        greet_around(t - 1)
-
-    @pl.when(t < nt - 1)
-    def _():
-        greet_around(t + 1)
 
     live_copy.wait()
     alive = lax.broadcasted_iota(jnp.int32, (chans, HOP), 0) < live[0]
@@ -629,8 +636,7 @@
             jnp.asarray(band_table()),
             jnp.asarray(lag_tables(segs * nt)),
         )
-        alive = jnp.arange(chans, dtype=jnp.int32)[:, None, None] < live_channels.reshape(1, 1, 1)
-        return jnp.where(alive, by_slot.transpose(1, 0, 2), F32(0.0))
+        return by_slot.transpose(1, 0, 2)
 
     in_specs = (P("chan", "tm"), P("chan"), P("chan", None))
     out_specs = P("chan", None, "tm")

time: 55.2 us -> 55.1 us (level)
  other arithmetic: 1.66 us -> 0 us
  local copies, waits for them, and re-layouts: 0 us -> 1.58 us
    select_n x1 -> x0, other arithmetic: 1.65 us -> none  [per_device(): return jnp.where(alive, by_slot.transpose(1, 0, 2), F32(0.0))]
    unnamed x0 -> x1, local copies, waits for them, and re-layouts: none -> 1.58 us
where the time goes in v5:
time: 55.1 us; the launch traced here: 54.9 us
  Pallas kernels  52.7 us (96%)
  local copies, waits for them, and re-layouts  1.58 us (3%)
  between operations  0.66 us (1%)
    pallas_call x1, Pallas kernels, per_device(): pl.pallas_call(functools.partial(kernel, nq, nt, segs, chans), out_shape=...  52.7 us
    unnamed x1, local copies, waits for them, and re-layouts  1.58 us

profile of v5, /device:TPU:1, one launch (start us, length us, event | category | flops | bytes accessed | tf_op | source)
XLA Modules:
  0.0 54.9 jit_solution(10913246775537664369)
XLA Ops:
  0.7 52.7 %shard_map.73 = f32[3,96,128]{2,1,0:T(8,128)} custom-call(s32[1]{0:T(128)S(6)} %copy.9.live_hbm, s32[1,3]{1,0:T(1,128)} %partners_hbm.1, bf16[96,8192]{1,0:T(8,128)(2,1)} %x_ref.1, f32[2,512]{1,0:T(2,128)} %constant.8.clone.taper_hbm, bf16[2,512,512]{2,1,0:T(8,128)(2,1)} %constant.9.clone.fwd_hbm, bf16[512,512]{1,0:T(8,128)(2,1)} %constant.10.clone.band_hbm, ...), custom_call_target="tpu_custom_call" | custom-call | tf_op jit(solution)/shard_map/pallas_call | solution.py:596
  53.4 1.6 %copy.10 = f32[96,3,128]{2,0,1:T(8,128)} copy(f32[96,3,128]{2,0,1:T(8,128)} %bitcast.1) | data formatting | bytes 294912

commit v6 on v5

--- a/solution.py
+++ b/solution.py
@@ -364,6 +364,8 @@
                 count, half, cols
             )
 
+    farthest = sorted(range(1, nt), key=lambda d: -min(d, nt - d))
+
     def exchange(group, first, count, d):
         peer = lax.rem(t + d, nt)
         return pltpu.make_async_remote_copy(
@@ -472,7 +474,7 @@
         )
 
     lags_of(0, 5)
-    for d in range(1, nt):
+    for d in farthest:
         exchange(0, 0, 5, d).start()
 
     first_white = jnp.where(c == 0, SLOT_E, SLOT_B)
@@ -490,7 +492,7 @@
         cross([(5, first_white, second_white)], first, count)
 
     lags_of(5, 1)
-    for d in range(1, nt):
+    for d in farthest:
         exchange(1, 5, 1, d).start()
 
     @pl.when(corner)

time: 55.1 us -> 55.9 us (1.015)
  Pallas kernels: 52.7 us -> 53.5 us
    pallas_call x1, Pallas kernels: 52.7 us -> 53.5 us  [per_device(): pl.pallas_call(functools.partial(kernel, nq, nt, segs, chans), out_shape=...]
where the time goes in v6:
time: 55.9 us; the launch traced here: 55.7 us
  Pallas kernels  53.5 us (96%)
  local copies, waits for them, and re-layouts  1.58 us (3%)
  between operations  0.66 us (1%)
    pallas_call x1, Pallas kernels, per_device(): pl.pallas_call(functools.partial(kernel, nq, nt, segs, chans), out_shape=...  53.5 us
    unnamed x1, local copies, waits for them, and re-layouts  1.58 us

profile of v6, /device:TPU:1, one launch (start us, length us, event | category | flops | bytes accessed | tf_op | source)
XLA Modules:
  0.0 55.7 jit_solution(5637598815156277189)
XLA Ops:
  0.7 53.5 %shard_map.73 = f32[3,96,128]{2,1,0:T(8,128)} custom-call(s32[1]{0:T(128)S(6)} %copy.9.live_hbm, s32[1,3]{1,0:T(1,128)} %partners_hbm.1, bf16[96,8192]{1,0:T(8,128)(2,1)} %x_ref.1, f32[2,512]{1,0:T(2,128)} %constant.8.clone.taper_hbm, bf16[2,512,512]{2,1,0:T(8,128)(2,1)} %constant.9.clone.fwd_hbm, bf16[512,512]{1,0:T(8,128)(2,1)} %constant.10.clone.band_hbm, ...), custom_call_target="tpu_custom_call" | custom-call | tf_op jit(solution)/shard_map/pallas_call | solution.py:598
  54.1 1.6 %copy.10 = f32[96,3,128]{2,0,1:T(8,128)} copy(f32[96,3,128]{2,0,1:T(8,128)} %bitcast.1) | data formatting | bytes 294912

commit v7 on v5

--- a/solution.py
+++ b/solution.py
@@ -443,15 +443,18 @@
         def _():
             arrive(SLOT_D, k)
 
+    main_left(0)
+    main_start(2)
     halo_wait(theirs)
     whiten([(theirs, 8, 8)])
     cross([(3, SLOT_B, SLOT_C)], 8, 8)
 
     for k in range(steps):
-        main_left(k)
-        if k + 2 < steps:
+        if k > 0:
+            main_left(k)
+        if 0 < k < steps - 2:
             main_start(k + 2)
-        else:
+        if k >= steps - 2:
             edge_start(2 * (k + 2 - steps))
             edge_start(2 * (k + 2 - steps) + 1)
         arrive_sides(k)

time: 55.1 us -> 55.1 us (level)
  no operation moved by 1% of the time
where the time goes in v7:
time: 55.1 us; the launch traced here: 54.9 us
  Pallas kernels  52.7 us (96%)
  local copies, waits for them, and re-layouts  1.58 us (3%)
  between operations  0.66 us (1%)
    pallas_call x1, Pallas kernels, per_device(): pl.pallas_call(functools.partial(kernel, nq, nt, segs, chans), out_shape=...  52.7 us
    unnamed x1, local copies, waits for them, and re-layouts  1.58 us

profile of v7, /device:TPU:1, one launch (start us, length us, event | category | flops | bytes accessed | tf_op | source)
XLA Modules:
  0.0 54.9 jit_solution(12877891487520439710)
XLA Ops:
  0.7 52.7 %shard_map.73 = f32[3,96,128]{2,1,0:T(8,128)} custom-call(s32[1]{0:T(128)S(6)} %copy.9.live_hbm, s32[1,3]{1,0:T(1,128)} %partners_hbm.1, bf16[96,8192]{1,0:T(8,128)(2,1)} %x_ref.1, f32[2,512]{1,0:T(2,128)} %constant.8.clone.taper_hbm, bf16[2,512,512]{2,1,0:T(8,128)(2,1)} %constant.9.clone.fwd_hbm, bf16[512,512]{1,0:T(8,128)(2,1)} %constant.10.clone.band_hbm, ...), custom_call_target="tpu_custom_call" | custom-call | tf_op jit(solution)/shard_map/pallas_call | solution.py:599
  53.4 1.6 %copy.10 = f32[96,3,128]{2,0,1:T(8,128)} copy(f32[96,3,128]{2,0,1:T(8,128)} %bitcast.1) | data formatting | bytes 294912
